TPU v7x, 128 devices: a whole 4x4x4 slice. The times are simulated.
128 devices in a mesh: pts: 32 (over y_hi, x, z), lev: 4 (over y_lo, core).
Axes of the slice: x: 4, y: 4 (y_hi: 2, y_lo: 2; y = y_hi * 2 + y_lo), z: 4, core: 2. Of those that a mesh axis runs over, the one named last changes fastest.
Arguments:
- members: bfloat16 [64, 32, 262144], P('pts', 'lev'), may hold values from -6 to 6
- gradient: float32 [32, 262144], P('lev', 'pts'), may hold values from -0.6 to 0.6
- horiz_loc: bfloat16 [32768, 128, 128], P(('pts', 'lev')), may hold values from 0 to 1
- vert_loc: bfloat16 [32768, 8, 128], P(('pts', 'lev')), may hold values from 0 to 1
- tile_block: int32 [32768], P(('pts', 'lev')), may hold values from 0 to 63
- tile_obs: int32 [32768], P(('pts', 'lev')), may hold values from 0 to 127, as said below
- tile_live: int32 [128], P(('pts', 'lev')), may hold values from 2 to 256, as said below
- obs_pert: bfloat16 [64, 16384], P(None, ('pts', 'lev')), may hold values from -6 to 6
- innovation: float32 [16384], P(('pts', 'lev')), may hold values from -6 to 6
- obs_error: float32 [16384], P(('pts', 'lev')), may hold values from 0.5 to 2
- obs_count: int32 [128], P(('pts', 'lev')), may hold values from 1 to 128, as said below
Outputs:
- sensitivity: float32 [16384], P(('pts', 'lev'))
- impact: float32 [16384], P(('pts', 'lev'))
Inputs may be any that keep to these rules, and one draw needn't show every extreme that they name: `tile_obs`: the device that owns observation block b is b // 1 in pts-major order; for every tile slot its pts index lies within 2 of the pts index of the slot's device, counted cyclically; every device's first two slots lie at the offsets 2 and minus 2. `tile_live`: slots of a device at positions below its count are live, the others are ignored; some device has all 256 live. `obs_count`: the live observations of a block are its first ones; some block is full.
All inputs are finite; a program needn't handle non-finite values.
Results may differ from a plain program's by a relative error of at most 0.0029.
Values may be sent and summed in bfloat16 or wider, within the bound.
A program may use at most 384 MiB of HBM per device.

v0:
```python
import functools

import jax
import jax.numpy as jnp
from jax import lax
from jax.experimental import pallas as pl
from jax.experimental.pallas import tpu as pltpu
from jax.sharding import PartitionSpec as P

MESH = pl.DeviceIdType.MESH
REACH = 2
N_PTS = 32
N_LEV = 4
SIZE = {"y": 2, "x": 4, "z": 4}
NAMES = ("y", "x", "z")
PARTS = ((0, 11), (11, 22), (22, 32))
WIDEST = 11
ORDERS = (("x", "z", "y"), ("z", "y", "x"), ("y", "x", "z"))
UNITS = tuple((k, a, b) for k in (0, 1) for a in (0, 1) for b in (0, 1))
LAG = 2
TILES = 256
GROUP = 16
SLOTS = 32


def distances(unit, axis):
    k, a, b = unit
    return {"y": (0, 1), "x": (a, a + 2), "z": (b, b + 2)}[axis]


def moves():
    count = 0
    for u, unit in enumerate(UNITS):
        for part in range(len(PARTS)):
            held = 1
            for axis in ORDERS[(part + u) % 3]:
                count += held * sum(1 for step in distances(unit, axis) if step)
                held *= 2
    return count


NEAR = [(o, r) for o in range(-REACH, REACH + 1) for r in range(N_LEV) if (o, r) != (0, 0)]


def kernel(
    members, gradient, horiz, vert, block_ref, owner_ref, live_ref, pert,
    out_ref,
    hop1, hop2, hop3, own, grad, tiles, vert_raw, vert_f, scaled, total,
    pert_raw, pert_f, pert_u, marks, select, rows, arrived,
    send_sem, recv_sem, near_send, near_recv, back_send, back_recv, local_sem,
):
    f32, bf16 = jnp.float32, jnp.bfloat16
    me, lev = lax.axis_index("pts"), lax.axis_index("lev")
    here = {"y": me // 16, "x": (me // 4) % 4, "z": me % 4}
    my_slot = (me * N_LEV + lev) % SLOTS

    def place(at):
        return at["y"] * 16 + at["x"] * 4 + at["z"]

    def moved(axis, step):
        at = dict(here)
        at[axis] = (at[axis] + step) % SIZE[axis]
        return place(at)

    local_copies = [
        pltpu.make_async_copy(horiz, tiles, local_sem.at[0]),
        pltpu.make_async_copy(gradient, grad, local_sem.at[1]),
        pltpu.make_async_copy(vert, vert_raw, local_sem.at[2]),
        pltpu.make_async_copy(pert, pert_raw.at[my_slot], local_sem.at[3]),
        pltpu.make_async_copy(
            members.at[:, here["y"], here["x"] // 2, here["x"] % 2, here["z"] // 2, here["z"] % 2],
            own,
            local_sem.at[4],
        ),
    ]

    barrier = pltpu.get_barrier_semaphore()
    line = [("x", 1), ("x", 2), ("x", 3), ("z", 1), ("z", 2), ("z", 3), ("y", 1)]
    for axis, step in line:
        pl.semaphore_signal(barrier, inc=1, device_id={"pts": moved(axis, step)}, device_id_type=MESH)
    near = [((me + o + N_PTS) % N_PTS, (lev + r) % N_LEV) for o, r in NEAR]
    for to in near:
        pl.semaphore_signal(barrier, inc=1, device_id=to, device_id_type=MESH)
    for copy in local_copies:
        copy.start()
    pl.semaphore_wait(barrier, len(line) + len(near))

    near_copies = []
    for i, to in enumerate(near):
        near_copies.append(
            pltpu.make_async_remote_copy(
                src_ref=pert,
                dst_ref=pert_raw.at[my_slot],
                send_sem=near_send.at[i],
                recv_sem=near_recv.at[i],
                device_id=to,
                device_id_type=MESH,
            )
        )

    hops = (hop1, hop2, hop3)
    held = {}
    sent = []

    def begin(u):
        k, a, b = UNITS[u]
        for part, (low, high) in enumerate(PARTS):
            base = members.at[
                k, :, :, (here["x"] + a) % 2, :, (here["z"] + b) % 2, pl.ds(low, high - low)
            ]
            held[u, part] = [({}, base, NAMES, None)]

    def settle(entry):
        if entry is not None and not entry[1]:
            entry[0].wait_recv()
            entry[1] = True

    def advance(u, part, stage, tick):
        low, high = PARTS[part]
        axis = ORDERS[(part + u) % 3][stage]
        fresh, slot = [], 0
        for moved_by, ref, left, entry in held[u, part]:
            settle(entry)
            for step in distances(UNITS[u], axis):
                target = (here[axis] + step) % SIZE[axis]
                index = target if axis == "y" else target // 2
                source = ref.at[tuple(index if n == axis else slice(None) for n in left)]
                rest = tuple(n for n in left if n != axis)
                by = {**moved_by, axis: step}
                if step == 0:
                    fresh.append((by, source, rest, entry))
                    continue
                there = hops[stage].at[
                    (u, part, slot) + (slice(None),) * len(rest) + (pl.ds(0, high - low),)
                ]
                copy = pltpu.make_async_remote_copy(
                    src_ref=source,
                    dst_ref=there,
                    send_sem=send_sem.at[len(sent)],
                    recv_sem=recv_sem.at[len(sent)],
                    device_id={"pts": moved(axis, step)},
                    device_id_type=MESH,
                )
                copy.start()
                sent.append((tick, copy))
                fresh.append((by, there, rest, [copy, False]))
                slot += 1
        held[u, part] = fresh


    def ready_local():
        for copy in local_copies:
            copy.wait()

    def turn_tiles(low, high):
        def body(i, carry):
            turned = [tiles[i * 4 + j].T for j in range(4)]
            for j in range(4):
                tiles[i * 4 + j] = turned[j]
            return carry

        lax.fori_loop(low // 4, high // 4, body, 0)

    def spread_vert():
        def body(i, carry):
            both = vert_raw[i].astype(f32)
            vert_f[2 * i] = both[:8]
            vert_f[2 * i + 1] = both[8:]
            return carry

        lax.fori_loop(0, TILES // 2, body, 0, unroll=4)

    def mark_owners(low, high):
        lanes = lax.broadcasted_iota(jnp.int32, (8, 128), 1)
        live = live_ref[0]

        def body(t, carry):
            slot = owner_ref[t] % SLOTS
            slot = jnp.where(t < live, slot, -1)
            marks[t] = jnp.where(lanes == slot, 1.0, 0.0).astype(f32)
            return carry

        lax.fori_loop(low, high, body, 0, unroll=8)

    def turn_marks():
        for i in range(TILES // GROUP):
            block = marks[i * GROUP:(i + 1) * GROUP].reshape(GROUP * 8, 128)
            select[i] = block.T[:SLOTS].astype(bf16)

    def spread_pert():
        for copy in near_copies:
            copy.wait()

        def body(s, carry):
            pert_f[s] = pert_raw[s].astype(f32)
            return carry

        lax.fori_loop(0, SLOTS, body, 0, unroll=2)

    def arrange(u):
        k = UNITS[u][0]
        for part in range(len(PARTS)):
            for item in held[u, part]:
                settle(item[3])
        order = [
            {"y": dy, "x": dx, "z": dz}
            for dy in distances(UNITS[u], "y")
            for dx in distances(UNITS[u], "x")
            for dz in distances(UNITS[u], "z")
        ]
        for i, by in enumerate(order):
            source = place({n: (here[n] - by[n] + SIZE[n]) % SIZE[n] for n in NAMES})
            pert_u[:, pl.ds(i, 1), :] = pert_f[:, pl.ds(source * 2 + k, 1), :]
        for part, (low, high) in enumerate(PARTS):
            refs = []
            for by in order:
                found = [item for item in held[u, part] if item[0] == by]
                ref = found[0][1]
                if not any(by.values()):
                    ref = own.at[k, pl.ds(low, high - low)]
                refs.append(ref)

            def body(j, carry, low=low, refs=refs):
                pair = low + j
                g = grad[pair]
                for i in range(0, len(refs), 2):
                    one = refs[i][j].astype(f32) * g
                    two = refs[i + 1][j].astype(f32) * g
                    scaled[2 * pair, i * 8:i * 8 + 16, :] = jnp.concatenate([one[:8], two[:8]], 0).astype(bf16)
                    scaled[2 * pair + 1, i * 8:i * 8 + 16, :] = jnp.concatenate([one[8:], two[8:]], 0).astype(bf16)
                return carry

            lax.fori_loop(0, high - low, body, 0)

    def scores(first):
        results = []
        left = [scaled[block_ref[first + i]] for i in range(GROUP)]
        right = [tiles[first + i] for i in range(GROUP)]
        products = [jnp.dot(left[i], right[i], preferred_element_type=f32) for i in range(GROUP)]
        for i in range(GROUP):
            weight = pert_u[owner_ref[first + i] % SLOTS]
            results.append(jnp.sum(products[i].reshape(8, 8, 128) * weight[:, None, :], axis=0))
        return results

    def work(u, low, high):
        def body(i, carry):
            first = i * GROUP
            results = scores(first)
            if u > 0:
                before = [total[first + j] for j in range(GROUP)]
                results = [results[j] + before[j] for j in range(GROUP)]
            for j in range(GROUP):
                total[first + j] = results[j]
            return carry

        lax.fori_loop(low, high, body, 0)

    def work_last():
        def body(i, carry):
            first = i * GROUP
            results = scores(first)
            results = [(results[j] + total[first + j]) * vert_f[first + j] for j in range(GROUP)]
            value = jnp.concatenate(results, axis=0)
            high = value.astype(bf16)
            low = (value - high.astype(f32)).astype(bf16)
            chosen = select[i]
            carry = carry + jnp.dot(chosen, high, preferred_element_type=f32)
            return carry + jnp.dot(chosen, low, preferred_element_type=f32)

        return lax.fori_loop(0, TILES // GROUP, body, jnp.zeros((SLOTS, 128), f32))

    jobs = [ready_local]
    jobs += [functools.partial(turn_tiles, i, i + 32) for i in range(0, TILES, 32)]
    jobs += [spread_vert]
    jobs += [functools.partial(mark_owners, i, i + 128) for i in range(0, TILES, 128)]
    jobs += [turn_marks, spread_pert]

    def next_job():
        if jobs:
            jobs.pop(0)()

    last = len(UNITS) - 1
    pending = 0
    for tick in range(last + 1 + 3 * LAG):
        if tick <= last:
            begin(tick)
        done = tick - 3 * LAG
        if done == 0:
            while jobs:
                next_job()
        if 0 <= done < last:
            jobs.append(functools.partial(arrange, done))
            pieces = TILES // GROUP // 4
            jobs += [functools.partial(work, done, i * pieces, (i + 1) * pieces) for i in range(4)]
        for part in range(len(PARTS)):
            for stage in (2, 1, 0):
                u = tick - stage * LAG
                if 0 <= u <= last:
                    advance(u, part, stage, tick)
                    if tick > 0:
                        next_job()
        if tick == 0:
            for copy in near_copies:
                copy.start()
        if done >= 0:
            while jobs:
                next_job()
        while pending < len(sent) and sent[pending][0] <= tick - 2:
            sent[pending][1].wait_send()
            pending += 1
    while pending < len(sent):
        sent[pending][1].wait_send()
        pending += 1
    arrange(last)
    sums = work_last()
    for s in range(SLOTS):
        rows[s] = sums[s:s + 1]
    back = []
    for i, to in enumerate(near):
        back.append(
            pltpu.make_async_remote_copy(
                src_ref=rows.at[(to[0] * N_LEV + to[1]) % SLOTS],
                dst_ref=arrived.at[i],
                send_sem=back_send.at[i],
                recv_sem=back_recv.at[i],
                device_id=to,
                device_id_type=MESH,
            )
        )
    for copy in back:
        copy.start()
    for copy in back:
        copy.wait_recv()
    whole = rows[my_slot]
    for i in range(len(NEAR)):
        whole = whole + arrived[i]
    out_ref[...] = whole
    for copy in back:
        copy.wait_send()


def local(
    members,
    gradient,
    horiz_loc,
    vert_loc,
    tile_block,
    tile_obs,
    tile_live,
    obs_pert,
    innovation,
    obs_error,
    obs_count,
):
    f32, bf16 = jnp.float32, jnp.bfloat16
    side = 128
    held, levels, columns = members.shape
    moving = members.reshape(held, levels, columns // side, side).transpose(0, 2, 1, 3)
    moving = moving.reshape(held, 2, 2, 2, 2, 2, 32, 16, side)
    slopes = gradient.reshape(levels, 64, side).transpose(1, 0, 2).reshape(32, 16, side)
    vertical = vert_loc.reshape(TILES // 2, 16, side)
    units, parts, count, close = len(UNITS), len(PARTS), moves(), len(NEAR)
    anywhere = pl.BlockSpec(memory_space=pl.ANY)
    scalar = pl.BlockSpec(memory_space=pltpu.SMEM)
    dma = pltpu.SemaphoreType.DMA
    raw_sum = pl.pallas_call(
        kernel,
        name="efsoi",
        out_shape=jax.ShapeDtypeStruct((1, side), f32),
        in_specs=[anywhere] * 4 + [scalar] * 3 + [anywhere],
        out_specs=pl.BlockSpec(memory_space=pltpu.VMEM),
        scratch_shapes=[
            pltpu.VMEM((units, parts, 2, 2, 2, WIDEST, 16, side), bf16),
            pltpu.VMEM((units, parts, 4, 2, WIDEST, 16, side), bf16),
            pltpu.VMEM((units, parts, 8, WIDEST, 16, side), bf16),
            pltpu.VMEM((2, 32, 16, side), bf16),
            pltpu.VMEM((32, 16, side), f32),
            pltpu.VMEM((TILES, side, side), bf16),
            pltpu.VMEM((TILES // 2, 16, side), bf16),
            pltpu.VMEM((TILES, 8, side), f32),
            pltpu.VMEM((64, 64, side), bf16),
            pltpu.VMEM((TILES, 8, side), f32),
            pltpu.VMEM((SLOTS, 64, side), bf16),
            pltpu.VMEM((SLOTS, 64, side), f32),
            pltpu.VMEM((SLOTS, 8, side), f32),
            pltpu.VMEM((TILES, 8, side), f32),
            pltpu.VMEM((TILES // GROUP, SLOTS, side), bf16),
            pltpu.VMEM((SLOTS, 1, side), f32),
            pltpu.VMEM((close, 1, side), f32),
            dma((count,)),
            dma((count,)),
            dma((close,)),
            dma((close,)),
            dma((close,)),
            dma((close,)),
            dma((5,)),
        ],
        compiler_params=pltpu.CompilerParams(
            collective_id=0, has_side_effects=True, vmem_limit_bytes=56 << 20
        ),
        cost_estimate=pl.CostEstimate(
            flops=2 * TILES * 512 * side * side, bytes_accessed=32 << 20, transcendentals=0
        ),
    )(moving, slopes, horiz_loc, vertical, tile_block, tile_obs, tile_live, obs_pert)
    sensitivity = raw_sum.reshape(side) / (64 - 1)
    observed = jnp.arange(side, dtype=jnp.int32) < obs_count[0]
    sensitivity = jnp.where(observed, sensitivity, jnp.zeros_like(sensitivity))
    impact = innovation * sensitivity / obs_error
    return (sensitivity, impact)


def solution(mesh):
    both = ("pts", "lev")
    placed = (
        P("pts", "lev", None),
        P("lev", "pts"),
        P(both, None, None),
        P(both, None, None),
        P(both),
        P(both),
        P(both),
        P(None, both),
        P(both),
        P(both),
        P(both),
    )
    return jax.shard_map(
        local,
        mesh=mesh,
        in_specs=placed,
        out_specs=(P(both), P(both)),
        check_vma=False,
    )
```

profile of v0, /device:TPU:1, one launch (start us, length us, event | category | flops | bytes accessed | tf_op | source)
XLA Modules:
  0.0 131.6 jit_solution(8672192886526465016)
XLA Ops:
  1.9 0.0 copy-start
  1.9 0.0 copy-start.1
  1.9 128.5 %efsoi.1 = f32[1,128]{1,0:T(1,128)} custom-call(bf16[2,2,2,2,2,2,32,16,128]{8,7,6,5,4,3,2,1,0:T(8,128)(2,1)} %bitcast.16, f32[32,16,128]{2,1,0:T(8,128)} %bitcast.18, bf16[256,128,128]{2,1,0:T(8,128)(2,1)} %horiz.1, bf16[128,16,128]{2,1,0:T(8,128)(2,1)} %bitcast.17, s32[256]{0:T(256)} %block_ref.1, s32[256]{0:T(256)} %owner_ref.1, s32[1]{0:T(128)S(6)} %copy.13.live_ref, ...), custom_call_target="tpu_custom_call" | custom-call | flops 4294967296 | bytes 33554432 | tf_op jit(solution)/shard_map/efsoi/pallas_call | solution.py:366
  130.4 0.0 copy-done
  130.4 0.0 copy-done.1
  130.4 1.2 multiply_divide_fusion
Async XLA Ops:
  1.9 128.5 %copy-start = (f32[128]{0:T(128)S(1)}, f32[128]{0:T(128)}, u32[]{:S(2)}) copy-start(f32[128]{0:T(128)} %param.20) | copy-start | bytes 1540
  1.9 128.5 %copy-start.1 = (f32[128]{0:T(128)S(1)}, f32[128]{0:T(128)}, u32[]{:S(2)}) copy-start(f32[128]{0:T(128)} %param.19) | copy-start | bytes 1540
where the time goes:
time: 132 us
  Pallas kernels  128 us (97%)
  between operations  1.97 us (1%)
    pallas_call x1, Pallas kernels, local(): pl.pallas_call(kernel, name='efsoi', out_shape=jax.ShapeDtypeStruct((1, s...  128 us

commit v1 on v0

--- a/solution.py
+++ b/solution.py
@@ -19,7 +19,8 @@
 UNITS = tuple((k, a, b) for k in (0, 1) for a in (0, 1) for b in (0, 1))
 LAG = 2
 TILES = 256
-GROUP = 16
+GROUP = 32
+LAST_GROUP = 64
 SLOTS = 32
 
 
@@ -47,12 +48,13 @@
     out_ref,
     hop1, hop2, hop3, own, grad, tiles, vert_raw, vert_f, scaled, total,
     pert_raw, pert_f, pert_u, marks, select, rows, arrived,
-    send_sem, recv_sem, near_send, near_recv, back_send, back_recv, local_sem,
+    send_sem, recv_sem, pert_send, pert_recv, back_send, back_recv, local_sem,
 ):
     f32, bf16 = jnp.float32, jnp.bfloat16
     me, lev = lax.axis_index("pts"), lax.axis_index("lev")
     here = {"y": me // 16, "x": (me // 4) % 4, "z": me % 4}
     my_slot = (me * N_LEV + lev) % SLOTS
+    chip, core = lev // 2, lev % 2
 
     def place(at):
         return at["y"] * 16 + at["x"] * 4 + at["z"]
@@ -66,7 +68,7 @@
         pltpu.make_async_copy(horiz, tiles, local_sem.at[0]),
         pltpu.make_async_copy(gradient, grad, local_sem.at[1]),
         pltpu.make_async_copy(vert, vert_raw, local_sem.at[2]),
-        pltpu.make_async_copy(pert, pert_raw.at[my_slot], local_sem.at[3]),
+        pltpu.make_async_copy(pert, pert_raw.at[chip, core, REACH], local_sem.at[3]),
         pltpu.make_async_copy(
             members.at[:, here["y"], here["x"] // 2, here["x"] % 2, here["z"] // 2, here["z"] % 2],
             own,
@@ -85,18 +87,22 @@
         copy.start()
     pl.semaphore_wait(barrier, len(line) + len(near))
 
-    near_copies = []
-    for i, to in enumerate(near):
-        near_copies.append(
-            pltpu.make_async_remote_copy(
-                src_ref=pert,
-                dst_ref=pert_raw.at[my_slot],
-                send_sem=near_send.at[i],
-                recv_sem=near_recv.at[i],
-                device_id=to,
-                device_id_type=MESH,
-            )
+    def pert_copy(i, source, there, to):
+        return pltpu.make_async_remote_copy(
+            src_ref=source,
+            dst_ref=there,
+            send_sem=pert_send.at[i],
+            recv_sem=pert_recv.at[i],
+            device_id=to,
+            device_id_type=MESH,
         )
+
+    pert_along = [
+        pert_copy(i, pert, pert_raw.at[chip, core, REACH - o], {"pts": (me + o + N_PTS) % N_PTS})
+        for i, o in enumerate((1, -1, 2, -2))
+    ]
+    pert_across = pert_copy(4, pert_raw.at[chip, core], pert_raw.at[chip, core], {"lev": (lev + 2) % N_LEV})
+    pert_beside = pert_copy(5, pert_raw.at[:, core], pert_raw.at[:, core], {"lev": lev + 1 - 2 * core})
 
     hops = (hop1, hop2, hop3)
     held = {}
@@ -183,41 +189,50 @@
         lax.fori_loop(low, high, body, 0, unroll=8)
 
     def turn_marks():
-        for i in range(TILES // GROUP):
-            block = marks[i * GROUP:(i + 1) * GROUP].reshape(GROUP * 8, 128)
-            select[i] = block.T[:SLOTS].astype(bf16)
+        for i in range(TILES // 16):
+            block = marks[i * 16:(i + 1) * 16].reshape(128, 128)
+            group, at = divmod(i, LAST_GROUP // 16)
+            select[group, :, at * 128:(at + 1) * 128] = block.T[:SLOTS].astype(bf16)
+
+    def pert_second():
+        for copy in pert_along:
+            copy.wait_recv()
+        pert_across.start()
+
+    def pert_third():
+        pert_across.wait_recv()
+        pert_beside.start()
 
     def spread_pert():
-        for copy in near_copies:
-            copy.wait()
-
-        def body(s, carry):
-            pert_f[s] = pert_raw[s].astype(f32)
-            return carry
-
-        lax.fori_loop(0, SLOTS, body, 0, unroll=2)
-
-    def arrange(u):
-        k = UNITS[u][0]
-        for part in range(len(PARTS)):
-            for item in held[u, part]:
-                settle(item[3])
-        order = [
+        pert_beside.wait_recv()
+        for copy in pert_along + [pert_across, pert_beside]:
+            copy.wait_send()
+        for o in range(-REACH, REACH + 1):
+            for r in range(N_LEV):
+                slot = (me + o + N_PTS) % (SLOTS // N_LEV) * N_LEV + r
+                pert_f[slot] = pert_raw[r // 2, r % 2, o + REACH].astype(f32)
+
+    def sources(u):
+        return [
             {"y": dy, "x": dx, "z": dz}
             for dy in distances(UNITS[u], "y")
             for dx in distances(UNITS[u], "x")
             for dz in distances(UNITS[u], "z")
         ]
-        for i, by in enumerate(order):
+
+    def order_pert(u):
+        for i, by in enumerate(sources(u)):
             source = place({n: (here[n] - by[n] + SIZE[n]) % SIZE[n] for n in NAMES})
-            pert_u[:, pl.ds(i, 1), :] = pert_f[:, pl.ds(source * 2 + k, 1), :]
+            pert_u[u, :, pl.ds(i, 1), :] = pert_f[:, pl.ds(source * 2 + UNITS[u][0], 1), :]
+
+    def arrange(u):
         for part, (low, high) in enumerate(PARTS):
             refs = []
-            for by in order:
-                found = [item for item in held[u, part] if item[0] == by]
-                ref = found[0][1]
+            for by in sources(u):
+                ref, entry = [(item[1], item[3]) for item in held[u, part] if item[0] == by][0]
+                settle(entry)
                 if not any(by.values()):
-                    ref = own.at[k, pl.ds(low, high - low)]
+                    ref = own.at[UNITS[u][0], pl.ds(low, high - low)]
                 refs.append(ref)
 
             def body(j, carry, low=low, refs=refs):
@@ -232,20 +247,20 @@
 
             lax.fori_loop(0, high - low, body, 0)
 
-    def scores(first):
+    def scores(u, first, size):
         results = []
-        left = [scaled[block_ref[first + i]] for i in range(GROUP)]
-        right = [tiles[first + i] for i in range(GROUP)]
-        products = [jnp.dot(left[i], right[i], preferred_element_type=f32) for i in range(GROUP)]
-        for i in range(GROUP):
-            weight = pert_u[owner_ref[first + i] % SLOTS]
+        left = [scaled[block_ref[first + i]] for i in range(size)]
+        right = [tiles[first + i] for i in range(size)]
+        products = [jnp.dot(left[i], right[i], preferred_element_type=f32) for i in range(size)]
+        for i in range(size):
+            weight = pert_u[u, owner_ref[first + i] % SLOTS]
             results.append(jnp.sum(products[i].reshape(8, 8, 128) * weight[:, None, :], axis=0))
         return results
 
     def work(u, low, high):
         def body(i, carry):
             first = i * GROUP
-            results = scores(first)
+            results = scores(u, first, GROUP)
             if u > 0:
                 before = [total[first + j] for j in range(GROUP)]
                 results = [results[j] + before[j] for j in range(GROUP)]
@@ -257,9 +272,9 @@
 
     def work_last():
         def body(i, carry):
-            first = i * GROUP
-            results = scores(first)
-            results = [(results[j] + total[first + j]) * vert_f[first + j] for j in range(GROUP)]
+            first = i * LAST_GROUP
+            results = scores(last, first, LAST_GROUP)
+            results = [(results[j] + total[first + j]) * vert_f[first + j] for j in range(LAST_GROUP)]
             value = jnp.concatenate(results, axis=0)
             high = value.astype(bf16)
             low = (value - high.astype(f32)).astype(bf16)
@@ -267,19 +282,20 @@
             carry = carry + jnp.dot(chosen, high, preferred_element_type=f32)
             return carry + jnp.dot(chosen, low, preferred_element_type=f32)
 
-        return lax.fori_loop(0, TILES // GROUP, body, jnp.zeros((SLOTS, 128), f32))
-
-    jobs = [ready_local]
-    jobs += [functools.partial(turn_tiles, i, i + 32) for i in range(0, TILES, 32)]
+        return lax.fori_loop(0, TILES // LAST_GROUP, body, jnp.zeros((SLOTS, 128), f32))
+
+    last = len(UNITS) - 1
+    turns = [functools.partial(turn_tiles, i, i + 32) for i in range(0, TILES, 32)]
+    jobs = [ready_local] + turns[:2] + [pert_second] + turns[2:7] + [pert_third] + turns[7:]
     jobs += [spread_vert]
     jobs += [functools.partial(mark_owners, i, i + 128) for i in range(0, TILES, 128)]
     jobs += [turn_marks, spread_pert]
+    jobs += [functools.partial(order_pert, u) for u in range(len(UNITS))]
 
     def next_job():
         if jobs:
             jobs.pop(0)()
 
-    last = len(UNITS) - 1
     pending = 0
     for tick in range(last + 1 + 3 * LAG):
         if tick <= last:
@@ -300,7 +316,7 @@
                     if tick > 0:
                         next_job()
         if tick == 0:
-            for copy in near_copies:
+            for copy in pert_along:
                 copy.start()
         if done >= 0:
             while jobs:
@@ -308,9 +324,6 @@
         while pending < len(sent) and sent[pending][0] <= tick - 2:
             sent[pending][1].wait_send()
             pending += 1
-    while pending < len(sent):
-        sent[pending][1].wait_send()
-        pending += 1
     arrange(last)
     sums = work_last()
     for s in range(SLOTS):
@@ -336,6 +349,8 @@
         whole = whole + arrived[i]
     out_ref[...] = whole
     for copy in back:
+        copy.wait_send()
+    for tick, copy in sent[pending:]:
         copy.wait_send()
 
 
@@ -380,17 +395,17 @@
             pltpu.VMEM((TILES, 8, side), f32),
             pltpu.VMEM((64, 64, side), bf16),
             pltpu.VMEM((TILES, 8, side), f32),
-            pltpu.VMEM((SLOTS, 64, side), bf16),
+            pltpu.VMEM((2, 2, 2 * REACH + 1, 64, side), bf16),
             pltpu.VMEM((SLOTS, 64, side), f32),
-            pltpu.VMEM((SLOTS, 8, side), f32),
+            pltpu.VMEM((units, SLOTS, 8, side), f32),
             pltpu.VMEM((TILES, 8, side), f32),
-            pltpu.VMEM((TILES // GROUP, SLOTS, side), bf16),
+            pltpu.VMEM((TILES // LAST_GROUP, SLOTS, LAST_GROUP * 8), bf16),
             pltpu.VMEM((SLOTS, 1, side), f32),
             pltpu.VMEM((close, 1, side), f32),
             dma((count,)),
             dma((count,)),
-            dma((close,)),
-            dma((close,)),
+            dma((6,)),
+            dma((6,)),
             dma((close,)),
             dma((close,)),
             dma((5,)),

time: 132 us -> 125 us (0.947)
  Pallas kernels: 128 us -> 121 us
    pallas_call x1, Pallas kernels: 128 us -> 121 us  [local(): pl.pallas_call(kernel, name='efsoi', out_shape=jax.ShapeDtypeStruct((1, s...]
where the time goes in v1:
time: 125 us; the launch traced here: 124 us
  Pallas kernels  121 us (97%)
  between operations  1.97 us (2%)
    pallas_call x1, Pallas kernels, local(): pl.pallas_call(kernel, name='efsoi', out_shape=jax.ShapeDtypeStruct((1, s...  121 us

profile of v1, /device:TPU:1, one launch (start us, length us, event | category | flops | bytes accessed | tf_op | source)
XLA Modules:
  0.0 124.4 jit_solution(3692793840534820732)
XLA Ops:
  1.9 0.0 copy-start
  1.9 0.0 copy-start.1
  1.9 121.3 %efsoi.1 = f32[1,128]{1,0:T(1,128)} custom-call(bf16[2,2,2,2,2,2,32,16,128]{8,7,6,5,4,3,2,1,0:T(8,128)(2,1)} %bitcast.16, f32[32,16,128]{2,1,0:T(8,128)} %bitcast.18, bf16[256,128,128]{2,1,0:T(8,128)(2,1)} %horiz.1, bf16[128,16,128]{2,1,0:T(8,128)(2,1)} %bitcast.17, s32[256]{0:T(256)} %block_ref.1, s32[256]{0:T(256)} %owner_ref.1, s32[1]{0:T(128)S(6)} %copy.13.live_ref, ...), custom_call_target="tpu_custom_call" | custom-call | flops 4294967296 | bytes 33554432 | tf_op jit(solution)/shard_map/efsoi/pallas_call | solution.py:381
  123.2 0.0 copy-done
  123.2 0.0 copy-done.1
  123.3 1.2 multiply_divide_fusion
Async XLA Ops:
  1.9 121.3 %copy-start = (f32[128]{0:T(128)S(1)}, f32[128]{0:T(128)}, u32[]{:S(2)}) copy-start(f32[128]{0:T(128)} %param.20) | copy-start | bytes 1540
  1.9 121.3 %copy-start.1 = (f32[128]{0:T(128)S(1)}, f32[128]{0:T(128)}, u32[]{:S(2)}) copy-start(f32[128]{0:T(128)} %param.19) | copy-start | bytes 1540

commit v2 on v1

--- a/solution.py
+++ b/solution.py
@@ -15,12 +15,15 @@
 NAMES = ("y", "x", "z")
 PARTS = ((0, 11), (11, 22), (22, 32))
 WIDEST = 11
-ORDERS = (("x", "z", "y"), ("z", "y", "x"), ("y", "x", "z"))
+ORDERS = (("x", "y", "z"), ("y", "z", "x"), ("z", "x", "y"))
 UNITS = tuple((k, a, b) for k in (0, 1) for a in (0, 1) for b in (0, 1))
 LAG = 2
+PASSES = ((0, 1), (2, 3), (4, 5), (6,), (7,))
+WIDTH = max(len(units) for units in PASSES)
 TILES = 256
+FLUSH = 12
 GROUP = 32
-LAST_GROUP = 64
+LAST_GROUP = 128
 SLOTS = 32
 
 
@@ -40,7 +43,7 @@
     return count
 
 
-NEAR = [(o, r) for o in range(-REACH, REACH + 1) for r in range(N_LEV) if (o, r) != (0, 0)]
+NEAR = [(o, r) for o in (2, -2, 1, -1, 0) for r in (2, 3, 1, 0) if (o, r) != (0, 0)]
 
 
 def kernel(
@@ -136,6 +139,7 @@
                 if step == 0:
                     fresh.append((by, source, rest, entry))
                     continue
+                assert slot < (2, 4, 8)[stage]
                 there = hops[stage].at[
                     (u, part, slot) + (slice(None),) * len(rest) + (pl.ds(0, high - low),)
                 ]
@@ -223,9 +227,13 @@
     def order_pert(u):
         for i, by in enumerate(sources(u)):
             source = place({n: (here[n] - by[n] + SIZE[n]) % SIZE[n] for n in NAMES})
-            pert_u[u, :, pl.ds(i, 1), :] = pert_f[:, pl.ds(source * 2 + UNITS[u][0], 1), :]
+            p, at = places[u]
+            pert_u[p, :, pl.ds(at * 8 + i, 1), :] = pert_f[:, pl.ds(source * 2 + UNITS[u][0], 1), :]
+
+    places = {u: (p, at) for p, units in enumerate(PASSES) for at, u in enumerate(units)}
 
     def arrange(u):
+        row = places[u][1] * 64
         for part, (low, high) in enumerate(PARTS):
             refs = []
             for by in sources(u):
@@ -235,33 +243,34 @@
                     ref = own.at[UNITS[u][0], pl.ds(low, high - low)]
                 refs.append(ref)
 
-            def body(j, carry, low=low, refs=refs):
+            def body(j, carry, low=low, refs=refs, row=row):
                 pair = low + j
                 g = grad[pair]
                 for i in range(0, len(refs), 2):
                     one = refs[i][j].astype(f32) * g
                     two = refs[i + 1][j].astype(f32) * g
-                    scaled[2 * pair, i * 8:i * 8 + 16, :] = jnp.concatenate([one[:8], two[:8]], 0).astype(bf16)
-                    scaled[2 * pair + 1, i * 8:i * 8 + 16, :] = jnp.concatenate([one[8:], two[8:]], 0).astype(bf16)
+                    scaled[2 * pair, row + i * 8:row + i * 8 + 16, :] = jnp.concatenate([one[:8], two[:8]], 0).astype(bf16)
+                    scaled[2 * pair + 1, row + i * 8:row + i * 8 + 16, :] = jnp.concatenate([one[8:], two[8:]], 0).astype(bf16)
                 return carry
 
             lax.fori_loop(0, high - low, body, 0)
 
-    def scores(u, first, size):
+    def scores(p, first, size):
         results = []
-        left = [scaled[block_ref[first + i]] for i in range(size)]
+        held_members = 8 * len(PASSES[p])
+        left = [scaled[block_ref[first + i], :8 * held_members] for i in range(size)]
         right = [tiles[first + i] for i in range(size)]
         products = [jnp.dot(left[i], right[i], preferred_element_type=f32) for i in range(size)]
         for i in range(size):
-            weight = pert_u[u, owner_ref[first + i] % SLOTS]
-            results.append(jnp.sum(products[i].reshape(8, 8, 128) * weight[:, None, :], axis=0))
+            weight = pert_u[p, owner_ref[first + i] % SLOTS, :held_members]
+            results.append(jnp.sum(products[i].reshape(held_members, 8, 128) * weight[:, None, :], axis=0))
         return results
 
-    def work(u, low, high):
+    def work(p, low, high):
         def body(i, carry):
             first = i * GROUP
-            results = scores(u, first, GROUP)
-            if u > 0:
+            results = scores(p, first, GROUP)
+            if p > 0:
                 before = [total[first + j] for j in range(GROUP)]
                 results = [results[j] + before[j] for j in range(GROUP)]
             for j in range(GROUP):
@@ -273,7 +282,7 @@
     def work_last():
         def body(i, carry):
             first = i * LAST_GROUP
-            results = scores(last, first, LAST_GROUP)
+            results = scores(len(PASSES) - 1, first, LAST_GROUP)
             results = [(results[j] + total[first + j]) * vert_f[first + j] for j in range(LAST_GROUP)]
             value = jnp.concatenate(results, axis=0)
             high = value.astype(bf16)
@@ -306,8 +315,9 @@
                 next_job()
         if 0 <= done < last:
             jobs.append(functools.partial(arrange, done))
-            pieces = TILES // GROUP // 4
-            jobs += [functools.partial(work, done, i * pieces, (i + 1) * pieces) for i in range(4)]
+            p, at = places[done]
+            if at == len(PASSES[p]) - 1:
+                jobs += [functools.partial(work, p, i, i + 1) for i in range(TILES // GROUP)]
         for part in range(len(PARTS)):
             for stage in (2, 1, 0):
                 u = tick - stage * LAG
@@ -318,7 +328,7 @@
         if tick == 0:
             for copy in pert_along:
                 copy.start()
-        if done >= 0:
+        if tick >= FLUSH:
             while jobs:
                 next_job()
         while pending < len(sent) and sent[pending][0] <= tick - 2:
@@ -393,11 +403,11 @@
             pltpu.VMEM((TILES, side, side), bf16),
             pltpu.VMEM((TILES // 2, 16, side), bf16),
             pltpu.VMEM((TILES, 8, side), f32),
-            pltpu.VMEM((64, 64, side), bf16),
+            pltpu.VMEM((64, WIDTH * 64, side), bf16),
             pltpu.VMEM((TILES, 8, side), f32),
             pltpu.VMEM((2, 2, 2 * REACH + 1, 64, side), bf16),
             pltpu.VMEM((SLOTS, 64, side), f32),
-            pltpu.VMEM((units, SLOTS, 8, side), f32),
+            pltpu.VMEM((len(PASSES), SLOTS, WIDTH * 8, side), f32),
             pltpu.VMEM((TILES, 8, side), f32),
             pltpu.VMEM((TILES // LAST_GROUP, SLOTS, LAST_GROUP * 8), bf16),
             pltpu.VMEM((SLOTS, 1, side), f32),

time: 125 us -> 122 us (0.976)
  Pallas kernels: 121 us -> 118 us
    pallas_call x1, Pallas kernels: 121 us -> 118 us  [local(): pl.pallas_call(kernel, name='efsoi', out_shape=jax.ShapeDtypeStruct((1, s...]
where the time goes in v2:
time: 122 us
  Pallas kernels  118 us (97%)
  between operations  1.97 us (2%)
    pallas_call x1, Pallas kernels, local(): pl.pallas_call(kernel, name='efsoi', out_shape=jax.ShapeDtypeStruct((1, s...  118 us

profile of v2, /device:TPU:1, one launch (start us, length us, event | category | flops | bytes accessed | tf_op | source)
XLA Modules:
  0.0 121.6 jit_solution(17951769446410991652)
XLA Ops:
  1.9 0.0 copy-start
  1.9 0.0 copy-start.1
  1.9 118.4 %efsoi.1 = f32[1,128]{1,0:T(1,128)} custom-call(bf16[2,2,2,2,2,2,32,16,128]{8,7,6,5,4,3,2,1,0:T(8,128)(2,1)} %bitcast.16, f32[32,16,128]{2,1,0:T(8,128)} %bitcast.18, bf16[256,128,128]{2,1,0:T(8,128)(2,1)} %horiz.1, bf16[128,16,128]{2,1,0:T(8,128)(2,1)} %bitcast.17, s32[256]{0:T(256)} %block_ref.1, s32[256]{0:T(256)} %owner_ref.1, s32[1]{0:T(128)S(6)} %copy.13.live_ref, ...), custom_call_target="tpu_custom_call" | custom-call | flops 4294967296 | bytes 33554432 | tf_op jit(solution)/shard_map/efsoi/pallas_call | solution.py:391
  120.3 0.0 copy-done
  120.4 0.0 copy-done.1
  120.4 1.2 multiply_divide_fusion
Async XLA Ops:
  1.9 118.4 %copy-start = (f32[128]{0:T(128)S(1)}, f32[128]{0:T(128)}, u32[]{:S(2)}) copy-start(f32[128]{0:T(128)} %param.20) | copy-start | bytes 1540
  1.9 118.4 %copy-start.1 = (f32[128]{0:T(128)S(1)}, f32[128]{0:T(128)}, u32[]{:S(2)}) copy-start(f32[128]{0:T(128)} %param.19) | copy-start | bytes 1540

commit v3 on v2

--- a/solution.py
+++ b/solution.py
@@ -16,7 +16,7 @@
 PARTS = ((0, 11), (11, 22), (22, 32))
 WIDEST = 11
 ORDERS = (("x", "y", "z"), ("y", "z", "x"), ("z", "x", "y"))
-UNITS = tuple((k, a, b) for k in (0, 1) for a in (0, 1) for b in (0, 1))
+UNITS = tuple((k, a, b) for a in (0, 1) for b in (0, 1) for k in (0, 1))
 LAG = 2
 PASSES = ((0, 1), (2, 3), (4, 5), (6,), (7,))
 WIDTH = max(len(units) for units in PASSES)

time: 122 us -> 121 us (level)
  no operation moved by 1% of the time
where the time goes in v3:
time: 121 us; the launch traced here: 120 us
  Pallas kernels  117 us (97%)
  between operations  1.97 us (2%)
    pallas_call x1, Pallas kernels, local(): pl.pallas_call(kernel, name='efsoi', out_shape=jax.ShapeDtypeStruct((1, s...  117 us

profile of v3, /device:TPU:1, one launch (start us, length us, event | category | flops | bytes accessed | tf_op | source)
XLA Modules:
  0.0 120.4 jit_solution(17151341113842134858)
XLA Ops:
  1.9 0.0 copy-start
  1.9 0.0 copy-start.1
  1.9 117.3 %efsoi.1 = f32[1,128]{1,0:T(1,128)} custom-call(bf16[2,2,2,2,2,2,32,16,128]{8,7,6,5,4,3,2,1,0:T(8,128)(2,1)} %bitcast.16, f32[32,16,128]{2,1,0:T(8,128)} %bitcast.18, bf16[256,128,128]{2,1,0:T(8,128)(2,1)} %horiz.1, bf16[128,16,128]{2,1,0:T(8,128)(2,1)} %bitcast.17, s32[256]{0:T(256)} %block_ref.1, s32[256]{0:T(256)} %owner_ref.1, s32[1]{0:T(128)S(6)} %copy.13.live_ref, ...), custom_call_target="tpu_custom_call" | custom-call | flops 4294967296 | bytes 33554432 | tf_op jit(solution)/shard_map/efsoi/pallas_call | solution.py:391
  119.2 0.0 copy-done
  119.2 0.0 copy-done.1
  119.2 1.2 multiply_divide_fusion
Async XLA Ops:
  1.9 117.3 %copy-start = (f32[128]{0:T(128)S(1)}, f32[128]{0:T(128)}, u32[]{:S(2)}) copy-start(f32[128]{0:T(128)} %param.20) | copy-start | bytes 1540
  1.9 117.3 %copy-start.1 = (f32[128]{0:T(128)S(1)}, f32[128]{0:T(128)}, u32[]{:S(2)}) copy-start(f32[128]{0:T(128)} %param.19) | copy-start | bytes 1540
